TPU v7x, 32 devices: a whole 2x2x4 slice. The times are simulated.
32 devices in a mesh: dp: 4 (over x, core), row: 4 (over z), col: 2 (over y).
Axes of the slice: x: 2, y: 2, z: 4, core: 2. Of those that a mesh axis runs over, the one named last changes fastest.
Arguments:
- x_in: bfloat16 [64, 197, 768], P(('dp', 'row'), None, 'col'), may hold values from -6 to 6
- cotangent: bfloat16 [64, 197, 768], P(('dp', 'row'), None, 'col'), may hold values from -6 to 6
- norm_gains: bfloat16 [2, 2, 768], P(None, None, 'col'), may hold values from 0.5 to 1.5
- norm_shifts: bfloat16 [2, 2, 768], P(None, None, 'col'), may hold values from -1.796875 to 1.796875
- w_qkv: bfloat16 [2, 3, 12, 64, 768], P(None, None, 'row', None, 'col'), may hold values from -0.21875 to 0.21875
- b_qkv: bfloat16 [2, 2, 12, 64], P(None, None, 'row'), may hold values from -3 to 3
- w_out: bfloat16 [2, 768, 768], P(None, 'row', 'col'), may hold values from -1.75 to 1.75
- out_biases: bfloat16 [2, 2, 768], P(None, None, 'col'), may hold values from -3 to 3
- w_up: bfloat16 [2, 768, 3072], P(None, 'col', 'row'), may hold values from -0.21875 to 0.21875
- b_up: bfloat16 [2, 3072], P(None, 'row'), may hold values from -3 to 3
- w_down: bfloat16 [2, 3072, 768], P(None, 'row', 'col'), may hold values from -0.109375 to 0.109375
Outputs:
- x_out: bfloat16 [64, 197, 768], P(('dp', 'row'), None, 'col')
- grad_input: float32 [64, 197, 768], P(('dp', 'row'), None, 'col')
- grad_norm_gains: float32 [2, 2, 768], P(None, None, 'col')
- grad_norm_shifts: float32 [2, 2, 768], P(None, None, 'col')
- grad_w_qkv: float32 [2, 3, 12, 64, 768], P(None, None, 'row', None, 'col')
- grad_b_qkv: float32 [2, 2, 12, 64], P(None, None, 'row')
- grad_w_out: float32 [2, 768, 768], P(None, 'row', 'col')
- grad_out_biases: float32 [2, 2, 768], P(None, None, 'col')
- grad_w_up: float32 [2, 768, 3072], P(None, 'col', 'row')
- grad_b_up: float32 [2, 3072], P(None, 'row')
- grad_w_down: float32 [2, 3072, 768], P(None, 'row', 'col')
All inputs are finite; a program needn't handle non-finite values.
Results may differ from a plain program's by a relative error of at most 0.023.
Values may be sent and summed in bfloat16 or wider, within the bound.
A program may use at most 192 MiB of HBM per device.

v0:
```python
import jax
import jax.numpy as jnp
from jax import lax
from jax.sharding import PartitionSpec as P

D = 768
HD = 64
LAYERS = 2


epsilon = 1e-06


def gelu_exact(values):
    return jax.nn.gelu(values, approximate=False)


def normalize(stream, norm_gain, shift):
    totals = lax.psum((jnp.sum(stream, axis=-1), jnp.sum(stream * stream, axis=-1)), "col")
    centre = totals[0][..., None] / D
    spread = totals[1][..., None] / D - centre * centre
    inv_scale = lax.rsqrt(spread + epsilon)
    unit_vals = (stream - centre) * inv_scale
    normed = (unit_vals * norm_gain + shift).astype(jnp.bfloat16)
    gathered = lax.all_gather(normed, "row", axis=0, tiled=True)
    return (gathered, normed, unit_vals, inv_scale)


def normalize_back(d_normed, unit_vals, inv_scale, norm_gain):
    d_gain = jnp.sum(d_normed * unit_vals, axis=(0, 1))
    d_shift = jnp.sum(d_normed, axis=(0, 1))
    d_unit = d_normed * norm_gain
    back_sums = lax.psum((jnp.sum(d_unit, axis=-1), jnp.sum(d_unit * unit_vals, axis=-1)), "col")
    d_input = inv_scale * (
        d_unit - back_sums[0][..., None] / D - unit_vals * back_sums[1][..., None] / D
    )
    return (d_input, d_gain, d_shift)


def gather_branch(values):
    return lax.all_gather(values, "col", axis=0, tiled=True)


def reduce_heads(partial_value):
    return lax.psum_scatter(
        partial_value.astype(jnp.bfloat16), "row", scatter_dimension=0, tiled=True
    ).astype(jnp.float32)


def gather_grads(values):
    return lax.all_gather(values, "row", axis=0, tiled=True)


def reduce_grad_width(partial_value):
    return lax.psum_scatter(
        partial_value.astype(jnp.bfloat16), "col", scatter_dimension=0, tiled=True
    ).astype(jnp.float32)


def gather_wide(values):
    return lax.all_gather(values, "col", axis=0, tiled=True)


def reduce_grad_heads(partial_value):
    return lax.psum_scatter(
        partial_value.astype(jnp.bfloat16), "row", scatter_dimension=0, tiled=True
    ).astype(jnp.float32)


def attend(query_h, key_h, value_h):
    scores = (
        jnp.einsum("bqhe,bkhe->bhqk", query_h, key_h, preferred_element_type=jnp.float32) * 0.125
    )
    row_max = jnp.max(scores, axis=-1, keepdims=True)
    exp_vals = jnp.exp(scores - row_max)
    exp_total = jnp.sum(exp_vals, axis=-1, keepdims=True)
    prob_vals = exp_vals / exp_total
    log_total = row_max + jnp.log(exp_total)
    mixture = jnp.einsum(
        "bhqk,bkhe->bqhe",
        prob_vals.astype(jnp.bfloat16),
        value_h,
        preferred_element_type=jnp.float32,
    )
    return (mixture.astype(jnp.bfloat16), log_total)


def attend_back(query_h, key_h, value_h, log_total, d_mix):
    scores = (
        jnp.einsum("bqhe,bkhe->bhqk", query_h, key_h, preferred_element_type=jnp.float32) * 0.125
    )
    prob_vals = jnp.exp(scores - log_total)
    d_value = jnp.einsum(
        "bhqk,bqhe->bkhe", prob_vals.astype(jnp.bfloat16), d_mix, preferred_element_type=jnp.float32
    )
    d_probs = jnp.einsum("bqhe,bkhe->bhqk", d_mix, value_h, preferred_element_type=jnp.float32)
    d_scores = (
        prob_vals * (d_probs - jnp.sum(prob_vals * d_probs, axis=-1, keepdims=True))
    ).astype(jnp.bfloat16)
    d_query = (
        jnp.einsum("bhqk,bkhe->bqhe", d_scores, key_h, preferred_element_type=jnp.float32) * 0.125
    )
    d_key = (
        jnp.einsum("bhqk,bqhe->bkhe", d_scores, query_h, preferred_element_type=jnp.float32) * 0.125
    )
    return jnp.stack([d_query, d_key, d_value], axis=2).astype(jnp.bfloat16)


def shards(
    x_in, cotangent, norm_gains, norm_shifts, w_qkv, b_qkv, w_out, out_biases, w_up, b_up, w_down
):
    stream = x_in.astype(jnp.float32)
    kept_values = []
    for layer_idx in range(LAYERS):
        gain_pair = norm_gains[layer_idx].astype(jnp.float32)
        shift_pair = norm_shifts[layer_idx].astype(jnp.float32)
        bias_pair = out_biases[layer_idx].astype(jnp.float32)
        weight_qkv = w_qkv[layer_idx]
        heads_local = weight_qkv.shape[1]
        flat_qkv = weight_qkv.reshape(-1, weight_qkv.shape[3])
        rows_a, normed_a, unit_a, scale_a = normalize(stream, gain_pair[0], shift_pair[0])
        summed = lax.psum_scatter(
            jnp.einsum("bsd,kd->bsk", rows_a, flat_qkv, preferred_element_type=jnp.float32).astype(
                jnp.bfloat16
            ),
            "col",
            scatter_dimension=0,
            tiled=True,
        ).astype(jnp.float32)
        summed = summed.reshape(summed.shape[0], summed.shape[1], 3, heads_local, HD)
        qkv_bias = b_qkv[layer_idx].astype(jnp.float32)
        bias_full = jnp.stack([qkv_bias[0], jnp.zeros_like(qkv_bias[0]), qkv_bias[1]])
        projected = (summed + bias_full).astype(jnp.bfloat16)
        mixture, log_total = attend(projected[:, :, 0], projected[:, :, 1], projected[:, :, 2])
        mixture = mixture.reshape(mixture.shape[0], mixture.shape[1], -1)
        gathered_mix = gather_branch(mixture)
        attended = (
            reduce_heads(
                jnp.dot(gathered_mix, w_out[layer_idx], preferred_element_type=jnp.float32)
            )
            + bias_pair[0]
        )
        stream = stream + attended
        rows_b, normed_b, unit_b, scale_b = normalize(stream, gain_pair[1], shift_pair[1])
        hidden = lax.psum_scatter(
            jnp.dot(rows_b, w_up[layer_idx], preferred_element_type=jnp.float32).astype(
                jnp.bfloat16
            ),
            "col",
            scatter_dimension=0,
            tiled=True,
        ).astype(jnp.float32)
        hidden = hidden + b_up[layer_idx].astype(jnp.float32)
        activated = gelu_exact(hidden).astype(jnp.bfloat16)
        gathered_act = gather_branch(activated)
        stream = (
            stream
            + reduce_heads(
                jnp.dot(gathered_act, w_down[layer_idx], preferred_element_type=jnp.float32)
            )
            + bias_pair[1]
        )
        kept_values.append(
            (
                unit_a,
                scale_a,
                rows_a,
                projected,
                log_total,
                gathered_mix,
                unit_b,
                scale_b,
                rows_b,
                hidden,
                gathered_act,
            )
        )
    result = stream.astype(jnp.bfloat16)
    d_stream = cotangent.astype(jnp.float32)
    layer_grads = [None] * LAYERS
    for layer_idx in reversed(range(LAYERS)):
        (
            unit_a,
            scale_a,
            rows_a,
            projected,
            log_total,
            gathered_mix,
            unit_b,
            scale_b,
            rows_b,
            hidden,
            gathered_act,
        ) = kept_values[layer_idx]
        gain_pair = norm_gains[layer_idx].astype(jnp.float32)
        weight_qkv = w_qkv[layer_idx]
        heads_local = weight_qkv.shape[1]
        flat_qkv = weight_qkv.reshape(-1, weight_qkv.shape[3])
        d_rows = gather_grads(d_stream.astype(jnp.bfloat16))
        d_bias_down = jnp.sum(d_rows, axis=(0, 1), dtype=jnp.float32)
        d_w_down = jnp.einsum(
            "bsf,bsd->fd", gathered_act, d_rows, preferred_element_type=jnp.float32
        )
        d_activated = reduce_grad_width(
            jnp.einsum("bsd,fd->bsf", d_rows, w_down[layer_idx], preferred_element_type=jnp.float32)
        )
        d_hidden = jax.vjp(gelu_exact, hidden)[1](d_activated)[0].astype(jnp.bfloat16)
        d_hidden_all = gather_wide(d_hidden)
        d_b_up = jnp.sum(d_hidden_all, axis=(0, 1), dtype=jnp.float32)
        d_w_up = jnp.einsum("bsd,bsf->df", rows_b, d_hidden_all, preferred_element_type=jnp.float32)
        d_normed = reduce_grad_heads(
            jnp.einsum(
                "bsf,df->bsd", d_hidden_all, w_up[layer_idx], preferred_element_type=jnp.float32
            )
        )
        d_input, d_gain_b, d_shift_b = normalize_back(d_normed, unit_b, scale_b, gain_pair[1])
        d_stream = d_stream + d_input
        d_rows = gather_grads(d_stream.astype(jnp.bfloat16))
        d_bias_out = jnp.sum(d_rows, axis=(0, 1), dtype=jnp.float32)
        d_w_out = jnp.einsum(
            "bsm,bsd->md", gathered_mix, d_rows, preferred_element_type=jnp.float32
        )
        d_mix = reduce_grad_width(
            jnp.einsum("bsd,md->bsm", d_rows, w_out[layer_idx], preferred_element_type=jnp.float32)
        ).astype(jnp.bfloat16)
        d_mix = d_mix.reshape(d_mix.shape[0], d_mix.shape[1], heads_local, HD)
        d_proj = attend_back(
            projected[:, :, 0], projected[:, :, 1], projected[:, :, 2], log_total, d_mix
        )
        d_proj_all = gather_wide(d_proj.reshape(d_proj.shape[0], d_proj.shape[1], -1))
        bias_sums = jnp.sum(d_proj_all, axis=(0, 1), dtype=jnp.float32).reshape(3, heads_local, HD)
        d_b_qkv = jnp.stack([bias_sums[0], bias_sums[2]])
        d_w_qkv = jnp.einsum(
            "bsk,bsd->kd", d_proj_all, rows_a, preferred_element_type=jnp.float32
        ).reshape(weight_qkv.shape)
        d_normed = reduce_grad_heads(
            jnp.einsum("bsk,kd->bsd", d_proj_all, flat_qkv, preferred_element_type=jnp.float32)
        )
        d_input, d_gain_a, d_shift_a = normalize_back(d_normed, unit_a, scale_a, gain_pair[0])
        d_stream = d_stream + d_input
        layer_grads[layer_idx] = (
            jnp.stack([d_gain_a, d_gain_b]),
            jnp.stack([d_shift_a, d_shift_b]),
            d_w_qkv,
            d_b_qkv,
            d_w_out,
            jnp.stack([d_bias_out, d_bias_down]),
            d_w_up,
            d_b_up,
            d_w_down,
        )
    stacked = [
        jnp.stack([layer_grads[layer_idx][member] for layer_idx in range(LAYERS)])
        for member in range(9)
    ]
    summed_params = (
        lax.psum(stacked[2].astype(jnp.bfloat16), "dp").astype(jnp.float32),
        lax.psum(stacked[3].astype(jnp.bfloat16), "dp").astype(jnp.float32),
        lax.psum(stacked[4].astype(jnp.bfloat16), "dp").astype(jnp.float32),
        lax.psum(stacked[5].astype(jnp.bfloat16), "dp").astype(jnp.float32),
        lax.psum(stacked[6].astype(jnp.bfloat16), "dp").astype(jnp.float32),
        lax.psum(stacked[7].astype(jnp.bfloat16), "dp").astype(jnp.float32),
        lax.psum(stacked[8].astype(jnp.bfloat16), "dp").astype(jnp.float32),
    )
    summed_norms = lax.psum((stacked[0], stacked[1]), ("dp", "row"))
    return (
        result,
        d_stream,
        summed_norms[0],
        summed_norms[1],
        summed_params[0],
        summed_params[1],
        summed_params[2],
        summed_params[3],
        summed_params[4],
        summed_params[5],
        summed_params[6],
    )


def solution(mesh):
    return jax.shard_map(
        shards,
        mesh=mesh,
        in_specs=(
            P(("dp", "row"), None, "col"),
            P(("dp", "row"), None, "col"),
            P(None, None, "col"),
            P(None, None, "col"),
            P(None, None, "row", None, "col"),
            P(None, None, "row", None),
            P(None, "row", "col"),
            P(None, None, "col"),
            P(None, "col", "row"),
            P(None, "row"),
            P(None, "row", "col"),
        ),
        out_specs=(
            P(("dp", "row"), None, "col"),
            P(("dp", "row"), None, "col"),
            P(None, None, "col"),
            P(None, None, "col"),
            P(None, None, "row", None, "col"),
            P(None, None, "row", None),
            P(None, "row", "col"),
            P(None, None, "col"),
            P(None, "col", "row"),
            P(None, "row"),
            P(None, "row", "col"),
        ),
        check_vma=False,
    )
```

profile of v0, /device:TPU:0, one launch (start us, length us, event | category | flops | bytes accessed | tf_op | source)
XLA Modules:
  0.0 2146.1 jit_solution(7391302332469346991)
XLA Ops:
  18.6 53.8 %all-gather.17.cloned.1.call-done = bf16[16,197,384]{2,1,0:T(8,128)(2,1)} async-done(((bf16[4,197,384]{2,1,0:T(8,128)(2,1)}), bf16[16,197,384]{2,1,0:T(8,128)(2,1)}) %all-gather.17.cloned.1.call-update) | async-done | bytes 2420752 | tf_op jit(solution)/shard_map/all_gather | solution.py:25
  81.4 101.4 %all-reduce.17.cloned.1.call-done = bf16[16,197,576]{2,0,1:T(8,128)(2,1)} async-done(((bf16[16,197,576]{2,0,1:T(8,128)(2,1)}), bf16[16,197,576]{2,0,1:T(8,128)(2,1)}) %all-reduce.17.cloned.1.call-update) | async-done | bytes 3631120
  232.6 49.6 %reduce-scatter.17.cloned.1.call-done = bf16[4,197,384]{2,1,0:T(8,128)(2,1)} async-done(((bf16[16,197,384]{2,1,0:T(8,128)(2,1)}), bf16[4,197,384]{2,1,0:T(8,128)(2,1)}) %reduce-scatter.17.cloned.1.call-update) | async-done | bytes 605200 | tf_op jit(solution)/shard_map/reduce_scatter | solution.py:45
  291.3 51.6 %all-gather.21.cloned.1.call-done = bf16[16,197,384]{2,1,0:T(8,128)(2,1)} async-done(((bf16[4,197,384]{2,1,0:T(8,128)(2,1)}), bf16[16,197,384]{2,1,0:T(8,128)(2,1)}) %all-gather.21.cloned.1.call-update) | async-done | bytes 2420752 | tf_op jit(solution)/shard_map/all_gather | solution.py:25
  350.2 60.4 %reduce-scatter.19.cloned.1.call-done = bf16[8,197,768]{2,1,0:T(8,128)(2,1)} async-done(((bf16[16,197,768]{2,1,0:T(8,128)(2,1)}), bf16[8,197,768]{2,1,0:T(8,128)(2,1)}) %reduce-scatter.19.cloned.1.call-update) | async-done | bytes 2420752 | tf_op jit(solution)/shard_map/reduce_scatter | solution.py:145
  425.4 64.2 %all-gather.23.cloned.1.call-done = bf16[16,197,768]{2,0,1:T(8,128)(2,1)} async-done(((bf16[8,197,768]{2,0,1:T(8,128)(2,1)}), bf16[16,197,768]{2,0,1:T(8,128)(2,1)}) %all-gather.23.cloned.1.call-update) | async-done | bytes 4841488 | tf_op jit(solution)/shard_map/all_gather | solution.py:41
  497.2 49.6 %reduce-scatter.21.cloned.1.call-done = bf16[4,197,384]{2,1,0:T(8,128)(2,1)} async-done(((bf16[16,197,384]{2,1,0:T(8,128)(2,1)}), bf16[4,197,384]{2,1,0:T(8,128)(2,1)}) %reduce-scatter.21.cloned.1.call-update) | async-done | bytes 605200 | tf_op jit(solution)/shard_map/reduce_scatter | solution.py:45
  555.0 51.4 %all-gather.25.cloned.1.call-done = bf16[16,197,384]{2,1,0:T(8,128)(2,1)} async-done(((bf16[4,197,384]{2,1,0:T(8,128)(2,1)}), bf16[16,197,384]{2,1,0:T(8,128)(2,1)}) %all-gather.25.cloned.1.call-update) | async-done | bytes 2420752 | tf_op jit(solution)/shard_map/all_gather | solution.py:25
  613.4 103.3 %all-reduce.19.cloned.1.call-done = bf16[16,197,576]{2,0,1:T(8,128)(2,1)} async-done(((bf16[16,197,576]{2,0,1:T(8,128)(2,1)}), bf16[16,197,576]{2,0,1:T(8,128)(2,1)}) %all-reduce.19.cloned.1.call-update) | async-done | bytes 3631120
  768.0 48.1 %reduce-scatter.23.cloned.1.call-done = bf16[4,197,384]{2,1,0:T(8,128)(2,1)} async-done(((bf16[16,197,384]{2,1,0:T(8,128)(2,1)}), bf16[4,197,384]{2,1,0:T(8,128)(2,1)}) %reduce-scatter.23.cloned.1.call-update) | async-done | bytes 605200 | tf_op jit(solution)/shard_map/reduce_scatter | solution.py:45
  823.7 46.2 %all-gather.33.cloned.1.call-done = bf16[16,197,384]{2,1,0:T(8,128)(2,1)} async-done(((bf16[4,197,384]{2,1,0:T(8,128)(2,1)}), bf16[16,197,384]{2,1,0:T(8,128)(2,1)}) %all-gather.33.cloned.1.call-update) | async-done | bytes 2420752 | tf_op jit(solution)/shard_map/all_gather | solution.py:51
  929.6 56.3 %reduce-scatter.29.cloned.1.call-done = bf16[8,197,768]{2,1,0:T(8,128)(2,1)} async-done(((bf16[16,197,768]{2,1,0:T(8,128)(2,1)}), bf16[8,197,768]{2,1,0:T(8,128)(2,1)}) %reduce-scatter.29.cloned.1.call-update) | async-done | bytes 2420752 | tf_op jit(solution)/shard_map/reduce_scatter | solution.py:55
  986.0 64.3 %reduce-scatter.25.cloned.1.call-done = bf16[8,197,768]{2,1,0:T(8,128)(2,1)} async-done(((bf16[16,197,768]{2,1,0:T(8,128)(2,1)}), bf16[8,197,768]{2,1,0:T(8,128)(2,1)}) %reduce-scatter.25.cloned.1.call-update) | async-done | bytes 2420752 | tf_op jit(solution)/shard_map/reduce_scatter | solution.py:145
  1066.4 64.2 %all-gather.35.cloned.1.call-done = bf16[16,197,768]{2,0,1:T(8,128)(2,1)} async-done(((bf16[8,197,768]{2,0,1:T(8,128)(2,1)}), bf16[16,197,768]{2,0,1:T(8,128)(2,1)}) %all-gather.35.cloned.1.call-update) | async-done | bytes 4841488 | tf_op jit(solution)/shard_map/all_gather | solution.py:61
  1138.4 49.7 %reduce-scatter.31.cloned.1.call-done = bf16[4,197,384]{2,1,0:T(8,128)(2,1)} async-done(((bf16[16,197,384]{2,1,0:T(8,128)(2,1)}), bf16[4,197,384]{2,1,0:T(8,128)(2,1)}) %reduce-scatter.31.cloned.1.call-update) | async-done | bytes 605200 | tf_op jit(solution)/shard_map/reduce_scatter | solution.py:65
  1198.1 51.8 %all-gather.37.cloned.1.call-done = bf16[16,197,384]{2,1,0:T(8,128)(2,1)} async-done(((bf16[4,197,384]{2,1,0:T(8,128)(2,1)}), bf16[16,197,384]{2,1,0:T(8,128)(2,1)}) %all-gather.37.cloned.1.call-update) | async-done | bytes 2420752 | tf_op jit(solution)/shard_map/all_gather | solution.py:51
  1302.7 49.2 %all-gather.39.cloned.1.call-done = bf16[16,197,576]{2,0,1:T(8,128)(2,1)} async-done(((bf16[8,197,576]{2,0,1:T(8,128)(2,1)}), bf16[16,197,576]{2,0,1:T(8,128)(2,1)}) %all-gather.39.cloned.1.call-update) | async-done | bytes 3631120 | tf_op jit(solution)/shard_map/all_gather | solution.py:61
  1358.6 59.0 %all-gather.31.cloned.1.call-done = bf16[16,197,768]{2,0,1:T(8,128)(2,1)} async-done(((bf16[8,197,768]{2,0,1:T(8,128)(2,1)}), bf16[16,197,768]{2,0,1:T(8,128)(2,1)}) %all-gather.31.cloned.1.call-update) | async-done | bytes 4841488 | tf_op jit(solution)/shard_map/all_gather | solution.py:41
  1524.7 51.8 %all-gather.41.cloned.1.call-done = bf16[16,197,384]{2,1,0:T(8,128)(2,1)} async-done(((bf16[4,197,384]{2,1,0:T(8,128)(2,1)}), bf16[16,197,384]{2,1,0:T(8,128)(2,1)}) %all-gather.41.cloned.1.call-update) | async-done | bytes 2420752 | tf_op jit(solution)/shard_map/all_gather | solution.py:51
  1583.3 61.0 %reduce-scatter.37.cloned.1.call-done = bf16[8,197,768]{2,1,0:T(8,128)(2,1)} async-done(((bf16[16,197,768]{2,1,0:T(8,128)(2,1)}), bf16[8,197,768]{2,1,0:T(8,128)(2,1)}) %reduce-scatter.37.cloned.1.call-update) | async-done | bytes 2420752 | tf_op jit(solution)/shard_map/reduce_scatter | solution.py:55
  1651.0 64.2 %all-gather.43.cloned.1.call-done = bf16[16,197,768]{2,0,1:T(8,128)(2,1)} async-done(((bf16[8,197,768]{2,0,1:T(8,128)(2,1)}), bf16[16,197,768]{2,0,1:T(8,128)(2,1)}) %all-gather.43.cloned.1.call-update) | async-done | bytes 4841488 | tf_op jit(solution)/shard_map/all_gather | solution.py:61
  1722.8 49.7 %reduce-scatter.39.cloned.1.call-done = bf16[4,197,384]{2,1,0:T(8,128)(2,1)} async-done(((bf16[16,197,384]{2,1,0:T(8,128)(2,1)}), bf16[4,197,384]{2,1,0:T(8,128)(2,1)}) %reduce-scatter.39.cloned.1.call-update) | async-done | bytes 605200 | tf_op jit(solution)/shard_map/reduce_scatter | solution.py:65
  1782.0 51.8 %all-gather.45.cloned.1.call-done = bf16[16,197,384]{2,1,0:T(8,128)(2,1)} async-done(((bf16[4,197,384]{2,1,0:T(8,128)(2,1)}), bf16[16,197,384]{2,1,0:T(8,128)(2,1)}) %all-gather.45.cloned.1.call-update) | async-done | bytes 2420752 | tf_op jit(solution)/shard_map/all_gather | solution.py:51
  2079.9 59.0 %all-reduce.2 = (f32[2,2,384]{2,1,0:T(2,128)}, f32[2,2,384]{2,1,0:T(2,128)}) all-reduce(f32[2,2,384]{2,1,0:T(2,128)S(1)} %pad_maximum_fusion.8, f32[2,2,384]{2,1,0:T(2,128)S(1)} %pad_maximum_fusion.9), channel_id=1, replica_groups=mesh['dp'=4,'row'=4,'col'=2] {'dp','row'}, use_global_device_ids=true, to_apply=%region_58.0 | all-reduce | flops 3072 | bytes 24576 | tf_op jit(solution)/shard_map/psum | solution.py:265
  (378 shorter events, 718.3 us)
Async XLA Ops:
  18.4 164.4 %all-reduce.17.cloned.1.call-start = ((), (), s32[]{:S(2)}) async-start(), calls=%async_computation.44 | async-start | bytes 8069120
  79.4 149.1 %all-gather.19.cloned.1.call-start = ((), (), s32[]{:S(2)}) async-start(), calls=%async_computation.15 | async-start | bytes 2359296 | tf_op jit(solution)/shard_map/all_gather | solution.py:41
  232.5 110.4 %all-gather.21.cloned.1.call-start = ((), (), s32[]{:S(2)}) async-start(), calls=%async_computation.17 | async-start | bytes 3072000 | tf_op jit(solution)/shard_map/all_gather | solution.py:25
  291.1 119.5 %reduce-scatter.19.cloned.1.call-start = ((), (), s32[]{:S(2)}) async-start(), calls=%async_computation.18 | async-start | bytes 7372800 | tf_op jit(solution)/shard_map/reduce_scatter | solution.py:145
  349.5 140.0 %all-gather.23.cloned.1.call-start = ((), (), s32[]{:S(2)}) async-start(), calls=%async_computation.19 | async-start | bytes 7262208 | tf_op jit(solution)/shard_map/all_gather | solution.py:41
  425.4 121.5 %reduce-scatter.21.cloned.1.call-start = ((), (), s32[]{:S(2)}) async-start(), calls=%async_computation.20 | async-start | bytes 3072000 | tf_op jit(solution)/shard_map/reduce_scatter | solution.py:45
  554.6 162.1 %all-reduce.19.cloned.1.call-start = ((), (), s32[]{:S(2)}) async-start(), calls=%async_computation.45 | async-start | bytes 8069120
  613.4 149.0 %all-gather.27.cloned.1.call-start = ((), (), s32[]{:S(2)}) async-start(), calls=%async_computation.22 | async-start | bytes 2359296 | tf_op jit(solution)/shard_map/all_gather | solution.py:41
  767.3 155.5 %all-gather.29.cloned.1.call-start = ((), (), s32[]{:S(2)}) async-start(), calls=%async_computation.24 | async-start | bytes 3072000 | tf_op jit(solution)/shard_map/all_gather | solution.py:25
  823.7 162.3 %reduce-scatter.29.cloned.1.call-start = ((), (), s32[]{:S(2)}) async-start(), calls=%async_computation.29 | async-start | bytes 7372800 | tf_op jit(solution)/shard_map/reduce_scatter | solution.py:55
  876.7 173.6 %reduce-scatter.25.cloned.1.call-start = ((), (), s32[]{:S(2)}) async-start(), calls=%async_computation.25 | async-start | bytes 7372800 | tf_op jit(solution)/shard_map/reduce_scatter | solution.py:145
  929.6 201.0 %all-gather.35.cloned.1.call-start = ((), (), s32[]{:S(2)}) async-start(), calls=%async_computation.30 | async-start | bytes 7262208 | tf_op jit(solution)/shard_map/all_gather | solution.py:61
  1066.4 121.7 %reduce-scatter.31.cloned.1.call-start = ((), (), s32[]{:S(2)}) async-start(), calls=%async_computation.31 | async-start | bytes 3072000 | tf_op jit(solution)/shard_map/reduce_scatter | solution.py:65
  1138.3 111.6 %all-gather.37.cloned.1.call-start = ((), (), s32[]{:S(2)}) async-start(), calls=%async_computation.32 | async-start | bytes 3072000 | tf_op jit(solution)/shard_map/all_gather | solution.py:51
  1296.8 120.8 %all-gather.31.cloned.1.call-start = ((), (), s32[]{:S(2)}) async-start(), calls=%async_computation.26 | async-start | bytes 7262208 | tf_op jit(solution)/shard_map/all_gather | solution.py:41
  1302.7 167.0 %reduce-scatter.35.cloned.1.call-start = ((), (), s32[]{:S(2)}) async-start(), calls=%async_computation.35 | async-start | bytes 3072000 | tf_op jit(solution)/shard_map/reduce_scatter | solution.py:65
  1358.4 162.6 %reduce-scatter.27.cloned.1.call-start = ((), (), s32[]{:S(2)}) async-start(), calls=%async_computation.27 | async-start | bytes 3072000 | tf_op jit(solution)/shard_map/reduce_scatter | solution.py:45
  1425.3 151.2 %all-gather.41.cloned.1.call-start = ((), (), s32[]{:S(2)}) async-start(), calls=%async_computation.36 | async-start | bytes 3072000 | tf_op jit(solution)/shard_map/all_gather | solution.py:51
  1524.7 119.7 %reduce-scatter.37.cloned.1.call-start = ((), (), s32[]{:S(2)}) async-start(), calls=%async_computation.37 | async-start | bytes 7372800 | tf_op jit(solution)/shard_map/reduce_scatter | solution.py:55
  1583.3 131.9 %all-gather.43.cloned.1.call-start = ((), (), s32[]{:S(2)}) async-start(), calls=%async_computation.38 | async-start | bytes 7262208 | tf_op jit(solution)/shard_map/all_gather | solution.py:61
  1651.0 121.5 %reduce-scatter.39.cloned.1.call-start = ((), (), s32[]{:S(2)}) async-start(), calls=%async_computation.39 | async-start | bytes 3072000 | tf_op jit(solution)/shard_map/reduce_scatter | solution.py:65
  1722.8 111.0 %all-gather.45.cloned.1.call-start = ((), (), s32[]{:S(2)}) async-start(), calls=%async_computation.40 | async-start | bytes 3072000 | tf_op jit(solution)/shard_map/all_gather | solution.py:51
  1880.7 137.0 %all-reduce.21.cloned.1.call-start = ((), (), s32[]{:S(2)}) async-start(), calls=%async_computation.46 | async-start | bytes 7077888 | tf_op jit(solution)/shard_map/psum | solution.py:257
  1942.0 127.5 %reduce-scatter.43.cloned.1.call-start = ((), (), s32[]{:S(2)}) async-start(), calls=%async_computation.43 | async-start | bytes 3072000 | tf_op jit(solution)/shard_map/reduce_scatter | solution.py:65
  (74 other events, 4600.4 us)
Sparse Core Ops, SparseCore 0:
  18.5 53.8 all-gather.16
  79.5 103.2 all-reduce.16
  291.2 51.6 all-gather.20
  349.7 60.8 reduce-scatter.18
  425.5 64.0 all-gather.22
  554.7 51.6 all-gather.24
  613.5 103.2 all-reduce.18
  818.2 51.6 all-gather.32
  871.9 50.8 all-gather.28
  925.0 60.8 reduce-scatter.28
  988.1 62.1 reduce-scatter.24
  1066.5 64.0 all-gather.34
  1138.5 49.5 reduce-scatter.30
  1198.2 51.6 all-gather.36
  1296.9 54.9 all-gather.38
  1353.5 64.0 all-gather.30
  1420.0 49.5 reduce-scatter.34
  1524.8 51.6 all-gather.40
  1583.4 60.8 reduce-scatter.36
  1651.1 64.0 all-gather.42
  1782.0 51.6 all-gather.44
  1880.8 54.9 all-gather.46
  1942.1 75.5 all-reduce.20
  2019.8 49.6 reduce-scatter.42
  (9 shorter events, 352.2 us)
where the time goes:
time: 2160 us; the launch traced here: 2150 us
  waiting for transfers between devices  1690 us (78%)
  matrix products  155 us (7%)
  other arithmetic  121 us (6%)
  blocking collectives  112 us (5%)
  local copies, waits for them, and re-layouts  48.8 us (2%)
    all_gather x4, waiting for transfers between devices, gather_wide(): return lax.all_gather(values, 'col', axis=0, tiled=True)  216 us
    unnamed x35, waiting for transfers between devices  205 us
    all_gather x4, waiting for transfers between devices, normalize(): gathered = lax.all_gather(normed, 'row', axis=0, tiled=True)  203 us
    all_gather x4, waiting for transfers between devices, gather_grads(): return lax.all_gather(values, 'row', axis=0, tiled=True)  202 us
    reduce_scatter x4, waiting for transfers between devices, reduce_heads(): lax.psum_scatter(partial_value.astype(jnp.bfloat16), 'row', scatter_dimen...  192 us
    reduce_scatter x4, waiting for transfers between devices, reduce_grad_heads(): lax.psum_scatter(partial_value.astype(jnp.bfloat16), 'row', scatter_dimen...  188 us
    all_gather x4, waiting for transfers between devices, gather_branch(): return lax.all_gather(values, 'col', axis=0, tiled=True)  179 us
    reduce_scatter x4, waiting for transfers between devices, reduce_grad_width(): lax.psum_scatter(partial_value.astype(jnp.bfloat16), 'col', scatter_dimen...  148 us
  transfers between devices with their start and end apart: 33, of which 33 were waited for; matrix products, arithmetic and copies ran while one was open for 5% of the time, Pallas kernels for 0%

commit v1 on v0

v1 whole, which is shorter than its diff:
```python
import functools

import jax
import jax.numpy as jnp
from jax import lax
from jax.sharding import PartitionSpec as P

HD = 64
LAYERS = 2
AXES = ("dp", "row", "col")
F32 = jnp.float32
BF16 = jnp.bfloat16


epsilon = 1e-06


def gelu_exact(values):
    return jax.nn.gelu(values, approximate=False)


def normalize(stream, norm_gain, shift):
    width = stream.shape[-1]
    centre = jnp.sum(stream, axis=-1, keepdims=True) / width
    spread = jnp.sum(stream * stream, axis=-1, keepdims=True) / width - centre * centre
    inv_scale = lax.rsqrt(spread + epsilon)
    unit_vals = (stream - centre) * inv_scale
    normed = (unit_vals * norm_gain + shift).astype(BF16)
    return normed, unit_vals, inv_scale


def normalize_back(d_normed, unit_vals, inv_scale, norm_gain):
    width = d_normed.shape[-1]
    d_gain = jnp.sum(d_normed * unit_vals, axis=0)
    d_shift = jnp.sum(d_normed, axis=0)
    d_unit = d_normed * norm_gain
    sum_one = jnp.sum(d_unit, axis=-1, keepdims=True)
    sum_two = jnp.sum(d_unit * unit_vals, axis=-1, keepdims=True)
    d_input = inv_scale * (d_unit - sum_one / width - unit_vals * (sum_two / width))
    return d_input, d_gain, d_shift


def matmul(spec, left, right):
    return jnp.einsum(spec, left, right, preferred_element_type=F32)


def shards(
    sizes,
    x_in,
    cotangent,
    norm_gains,
    norm_shifts,
    w_qkv,
    b_qkv,
    w_out,
    out_biases,
    w_up,
    b_up,
    w_down,
):
    n_dp, n_row, n_col = sizes
    my_dp = lax.axis_index("dp")
    my_row = lax.axis_index("row")
    my_col = lax.axis_index("col")
    heads_local = w_qkv.shape[2]
    heads = heads_local * n_row
    wide = x_in.shape[-1]
    width = wide * n_col
    part_e = HD // n_dp
    part_m = w_out.shape[1] // n_dp
    part_f = w_down.shape[1] // n_dp
    rows_qkv = 3 * heads_local * part_e
    hidden_units = w_down.shape[1] * n_row

    def part(values, size, axis):
        return lax.dynamic_slice_in_dim(values, my_dp * size, size, axis)

    small = jnp.concatenate(
        [
            norm_gains.reshape(-1, wide),
            norm_shifts.reshape(-1, wide),
            out_biases.reshape(-1, wide),
        ]
    )
    small_rows = jnp.concatenate([b_qkv.reshape(-1), b_up.reshape(-1)])
    n_small = small.shape[0]
    n_side = -(-small_rows.shape[0] // wide)
    side_pad = n_side * wide - small_rows.shape[0]
    small_rows = jnp.pad(small_rows, (0, side_pad)).reshape(n_side, wide)

    def gather_attn(layer):
        pieces = [
            part(w_qkv[layer], part_e, 2).reshape(rows_qkv, wide),
            part(w_out[layer], part_m, 0),
        ]
        if layer == 0:
            pieces += [small, small_rows]
        packed = jnp.concatenate(pieces)
        got = lax.all_gather(packed, AXES, axis=0, tiled=False)
        return got.reshape(n_dp, n_row, n_col, -1, wide)

    def gather_ff(layer):
        packed = jnp.concatenate(
            [part(w_up[layer].T, part_f, 0), part(w_down[layer], part_f, 0)]
        )
        got = lax.all_gather(packed, AXES, axis=0, tiled=False)
        return got.reshape(n_dp, n_row, n_col, -1, wide)

    def whole_rows(got):
        return got.transpose(1, 0, 3, 2, 4).reshape(-1, width)

    def whole_qkv(got):
        got = got.reshape(n_dp, n_row, n_col, 3, heads_local, part_e, wide)
        return got.transpose(3, 1, 4, 0, 5, 2, 6).reshape(3, heads * HD, width)

    def cut_rows(grad, size):
        grad = grad.astype(BF16).reshape(n_row, n_dp, size, n_col, wide)
        return grad.transpose(1, 0, 3, 2, 4).reshape(-1, size, wide)

    def cut_qkv(grad):
        grad = grad.astype(BF16).reshape(3, n_row, heads_local, n_dp, part_e, n_col, wide)
        return grad.transpose(3, 1, 5, 0, 2, 4, 6).reshape(-1, rows_qkv, wide)

    def spread_sum(cuts):
        packed = jnp.concatenate(cuts, axis=1)
        return lax.psum_scatter(packed, AXES, scatter_dimension=0, tiled=False)

    tokens = x_in.shape[1]
    padded = -(-tokens // 16) * 16

    def to_images(values):
        both = lax.all_to_all(values, "col", split_axis=1, concat_axis=3, tiled=True)
        return jnp.pad(both, ((0, 0), (0, 0), (0, padded - tokens), (0, 0)))

    def to_blocks(values):
        values = values.astype(BF16).reshape(-1, padded, width)[:, :tokens]
        return lax.all_to_all(values, "col", split_axis=2, concat_axis=0, tiled=True)

    got_attn = [gather_attn(layer) for layer in range(LAYERS)]
    got_ff = [gather_ff(layer) for layer in range(LAYERS)]
    streams = to_images(jnp.stack([x_in, cotangent]))
    images = streams.shape[1]
    stream = streams[0].reshape(-1, width).astype(F32)

    cut_a = rows_qkv + part_m
    got_small = got_attn[0][0, 0, :, cut_a : cut_a + n_small]
    got_small = got_small.transpose(1, 0, 2).reshape(3, LAYERS, 2, width).astype(F32)
    gains, shifts, biases = got_small[0], got_small[1], got_small[2]
    got_side = got_attn[0][0, :, 0, cut_a + n_small :].reshape(n_row, -1)
    n_bqkv = b_qkv.size
    bias_qkv = got_side[:, :n_bqkv].reshape(n_row, LAYERS, 2, heads_local * HD)
    bias_qkv = bias_qkv.transpose(1, 2, 0, 3).reshape(LAYERS, 2, heads * HD).astype(F32)
    bias_up = got_side[:, n_bqkv : n_bqkv + b_up.size].reshape(n_row, LAYERS, -1)
    bias_up = bias_up.transpose(1, 0, 2).reshape(LAYERS, hidden_units).astype(F32)

    key_mask = jnp.arange(padded) < tokens

    def split_heads(values):
        return values.reshape(images, padded, heads, HD).transpose(0, 2, 1, 3)

    def join_heads(values):
        return values.transpose(0, 2, 1, 3).reshape(images * padded, heads * HD)

    kept_values = []
    for layer in range(LAYERS):
        weight_qkv = whole_qkv(got_attn[layer][..., :rows_qkv, :])
        weight_out = whole_rows(got_attn[layer][..., rows_qkv:cut_a, :])
        normed_a, unit_a, scale_a = normalize(stream, gains[layer, 0], shifts[layer, 0])
        query_h = matmul("td,kd->tk", normed_a, weight_qkv[0]) + bias_qkv[layer, 0]
        key_h = matmul("td,kd->tk", normed_a, weight_qkv[1])
        value_h = matmul("td,kd->tk", normed_a, weight_qkv[2]) + bias_qkv[layer, 1]
        query_h, key_h, value_h = (
            split_heads(v.astype(BF16)) for v in (query_h, key_h, value_h)
        )
        scores = matmul("bhqe,bhke->bhqk", query_h, key_h) * 0.125
        scores = jnp.where(key_mask, scores, -jnp.inf)
        row_max = jnp.max(scores, axis=-1, keepdims=True)
        exp_vals = jnp.exp(scores - row_max)
        probs = exp_vals / jnp.sum(exp_vals, axis=-1, keepdims=True)
        mixture = join_heads(
            matmul("bhqk,bhke->bhqe", probs.astype(BF16), value_h).astype(BF16)
        )
        stream = stream + (matmul("tm,md->td", mixture, weight_out) + biases[layer, 0])
        normed_b, unit_b, scale_b = normalize(stream, gains[layer, 1], shifts[layer, 1])
        weight_up = whole_rows(got_ff[layer][..., :part_f, :])
        weight_down = whole_rows(got_ff[layer][..., part_f:, :])
        hidden = matmul("td,fd->tf", normed_b, weight_up) + bias_up[layer]
        activated = gelu_exact(hidden).astype(BF16)
        stream = stream + (matmul("tf,fd->td", activated, weight_down) + biases[layer, 1])
        kept_values.append(
            (
                (weight_qkv, weight_out, weight_up, weight_down),
                (normed_a, unit_a, scale_a),
                (query_h, key_h, value_h, probs, mixture),
                (normed_b, unit_b, scale_b),
                (hidden, activated),
            )
        )

    result = to_blocks(stream)
    d_stream = streams[1].reshape(-1, width).astype(F32)
    small_grads = [None] * LAYERS
    sums_attn = [None] * LAYERS
    sums_ff = [None] * LAYERS
    for layer in reversed(range(LAYERS)):
        weights, norm_a, attn, norm_b, ff = kept_values[layer]
        weight_qkv, weight_out, weight_up, weight_down = weights
        normed_a, unit_a, scale_a = norm_a
        query_h, key_h, value_h, probs, mixture = attn
        normed_b, unit_b, scale_b = norm_b
        hidden, activated = ff
        d_rows = d_stream.astype(BF16)
        d_bias_down = jnp.sum(d_rows, axis=0, dtype=F32)
        d_w_down = matmul("tf,td->fd", activated, d_rows)
        d_activated = matmul("td,fd->tf", d_rows, weight_down)
        d_hidden = jax.vjp(gelu_exact, hidden)[1](d_activated)[0].astype(BF16)
        d_b_up = jnp.sum(d_hidden, axis=0, dtype=F32)
        d_w_up = matmul("tf,td->fd", d_hidden, normed_b)
        sums_ff[layer] = spread_sum([cut_rows(d_w_up, part_f), cut_rows(d_w_down, part_f)])
        d_normed = matmul("tf,fd->td", d_hidden, weight_up)
        d_input, d_gain_b, d_shift_b = normalize_back(d_normed, unit_b, scale_b, gains[layer, 1])
        d_stream = d_stream + d_input
        d_rows = d_stream.astype(BF16)
        d_bias_out = jnp.sum(d_rows, axis=0, dtype=F32)
        d_w_out = matmul("tm,td->md", mixture, d_rows)
        d_mix = split_heads(matmul("td,md->tm", d_rows, weight_out).astype(BF16))
        d_value = matmul("bhqk,bhqe->bhke", probs.astype(BF16), d_mix)
        d_probs = matmul("bhqe,bhke->bhqk", d_mix, value_h)
        d_scores = (
            probs * (d_probs - jnp.sum(probs * d_probs, axis=-1, keepdims=True))
        ).astype(BF16)
        d_query = matmul("bhqk,bhke->bhqe", d_scores, key_h) * 0.125
        d_key = matmul("bhqk,bhqe->bhke", d_scores, query_h) * 0.125
        d_query, d_key, d_value = (
            join_heads(v.astype(BF16)) for v in (d_query, d_key, d_value)
        )
        d_b_qkv = jnp.stack(
            [jnp.sum(d_query, axis=0, dtype=F32), jnp.sum(d_value, axis=0, dtype=F32)]
        )
        d_w_qkv = jnp.stack(
            [matmul("tk,td->kd", v, normed_a) for v in (d_query, d_key, d_value)]
        )
        sums_attn[layer] = spread_sum([cut_qkv(d_w_qkv), cut_rows(d_w_out, part_m)])
        d_normed = (
            matmul("tk,kd->td", d_query, weight_qkv[0])
            + matmul("tk,kd->td", d_key, weight_qkv[1])
            + matmul("tk,kd->td", d_value, weight_qkv[2])
        )
        d_input, d_gain_a, d_shift_a = normalize_back(d_normed, unit_a, scale_a, gains[layer, 0])
        d_stream = d_stream + d_input
        small_grads[layer] = (
            jnp.stack([d_gain_a, d_gain_b]),
            jnp.stack([d_shift_a, d_shift_b]),
            jnp.stack([d_bias_out, d_bias_down]),
            d_b_qkv,
            d_b_up,
        )

    stacked = [jnp.stack([small_grads[layer][m] for layer in range(LAYERS)]) for m in range(5)]
    summed = lax.psum(jnp.concatenate([s.reshape(-1) for s in stacked]), AXES)
    ends = []
    start = 0
    for member in stacked:
        ends.append(summed[start : start + member.size].reshape(member.shape))
        start += member.size

    def my_cols(values):
        return lax.dynamic_slice_in_dim(values, my_col * wide, wide, 2)

    def my_rows(values):
        size = values.shape[-1] // n_row
        return lax.dynamic_slice_in_dim(values, my_row * size, size, values.ndim - 1)

    gains_grad, shifts_grad, biases_grad = (my_cols(v) for v in ends[:3])
    b_qkv_grad = my_rows(ends[3]).reshape(b_qkv.shape)
    b_up_grad = my_rows(ends[4])

    def over_dp(values):
        return lax.all_gather(values, "dp", axis=0, tiled=False)

    out_qkv, out_out, out_up, out_down = [], [], [], []
    for layer in range(LAYERS):
        attn_sum = over_dp(sums_attn[layer]).astype(F32)
        ff_sum = over_dp(sums_ff[layer]).astype(F32)
        qkv_sum = attn_sum[:, :rows_qkv].reshape(n_dp, 3, heads_local, part_e, wide)
        out_qkv.append(qkv_sum.transpose(1, 2, 0, 3, 4).reshape(w_qkv.shape[1:]))
        out_out.append(attn_sum[:, rows_qkv:].reshape(-1, wide))
        out_up.append(ff_sum[:, :part_f].reshape(-1, wide).T)
        out_down.append(ff_sum[:, part_f:].reshape(-1, wide))

    return (
        result,
        to_blocks(d_stream).astype(F32),
        gains_grad,
        shifts_grad,
        jnp.stack(out_qkv),
        b_qkv_grad,
        jnp.stack(out_out),
        biases_grad,
        jnp.stack(out_up),
        b_up_grad,
        jnp.stack(out_down),
    )


def solution(mesh):
    sizes = tuple(mesh.shape[axis] for axis in AXES)
    return jax.shard_map(
        functools.partial(shards, sizes),
        mesh=mesh,
        in_specs=(
            P(("dp", "row"), None, "col"),
            P(("dp", "row"), None, "col"),
            P(None, None, "col"),
            P(None, None, "col"),
            P(None, None, "row", None, "col"),
            P(None, None, "row", None),
            P(None, "row", "col"),
            P(None, None, "col"),
            P(None, "col", "row"),
            P(None, "row"),
            P(None, "row", "col"),
        ),
        out_specs=(
            P(("dp", "row"), None, "col"),
            P(("dp", "row"), None, "col"),
            P(None, None, "col"),
            P(None, None, "col"),
            P(None, None, "row", None, "col"),
            P(None, None, "row", None),
            P(None, "row", "col"),
            P(None, None, "col"),
            P(None, "col", "row"),
            P(None, "row"),
            P(None, "row", "col"),
        ),
        check_vma=False,
    )
```

time: 2160 us -> 1160 us (0.54)
  waiting for transfers between devices: 1690 us -> 634 us
  local copies, waits for them, and re-layouts: 48.8 us -> 287 us
  blocking collectives: 112 us -> 15.3 us
  other arithmetic: 121 us -> 44.7 us
    all_gather x16 -> x6, waiting for transfers between devices: 799 us -> 197 us  [the longest x2 92.4 us: gather_ff(): got = lax.all_gather(packed, AXES, axis=0, tiled=False)]
    reduce_scatter x14 -> x4, waiting for transfers between devices: 653 us -> 287 us  [spread_sum(): return lax.psum_scatter(packed, AXES, scatter_dimension=0, tiled=False)]
    unnamed x35 -> x11, waiting for transfers between devices: 205 us -> 0.67 us
    psum x10 -> x0, blocking collectives: 112 us -> none  [the longest x1 59 us: shards(): summed_norms = lax.psum((stacked[0], stacked[1]), ('dp', 'row'))]
    psum x1, waiting for transfers between devices: 33.2 us -> 124 us  [shards(): summed = lax.psum(jnp.concatenate([s.reshape(-1) for s in stacked]), AXES)]
    unnamed x135 -> x278, local copies, waits for them, and re-layouts: 10.5 us -> 98 us
    reshape x2 -> x41, local copies, waits for them, and re-layouts: 11.8 us -> 99.1 us  [the longest x12 68.1 us: cut_rows(): grad = grad.astype(BF16).reshape(n_row, n_dp, size, n_col, wide)]
    convert_element_type x27 -> x9, other arithmetic: 69.2 us -> 6.64 us  [the longest x2 2.32 us: shards(): d_scores = (probs * (d_probs - jnp.sum(probs * d_probs, axis=-1, keepdims...]
  transfers between devices with their start and end apart: 33 -> 14, of which waited for: 33 -> 12; matrix products, arithmetic and copies ran while one was open for 5% -> 25% of each run, Pallas kernels for 0% -> 0%
where the time goes in v1:
time: 1160 us; the launch traced here: 1150 us
  waiting for transfers between devices  634 us (55%)
  local copies, waits for them, and re-layouts  287 us (25%)
  matrix products  145 us (12%)
  other arithmetic  44.7 us (4%)
  between operations  16.7 us (1%)
  blocking collectives  15.3 us (1%)
  starting transfers between devices  12.1 us (1%)
    reduce_scatter x4, waiting for transfers between devices, spread_sum(): return lax.psum_scatter(packed, AXES, scatter_dimension=0, tiled=False)  287 us
    dot_general x48, matrix products, matmul(): return jnp.einsum(spec, left, right, preferred_element_type=F32)  145 us
    psum x1, waiting for transfers between devices, shards(): summed = lax.psum(jnp.concatenate([s.reshape(-1) for s in stacked]), AXES)  124 us
    unnamed x278, local copies, waits for them, and re-layouts  98 us
    all_gather x2, waiting for transfers between devices, gather_ff(): got = lax.all_gather(packed, AXES, axis=0, tiled=False)  92.4 us
    all_gather x2, waiting for transfers between devices, gather_attn(): got = lax.all_gather(packed, AXES, axis=0, tiled=False)  79.7 us
    reshape x12, local copies, waits for them, and re-layouts, cut_rows(): grad = grad.astype(BF16).reshape(n_row, n_dp, size, n_col, wide)  68.1 us
    all_gather x2, waiting for transfers between devices, over_dp(): return lax.all_gather(values, 'dp', axis=0, tiled=False)  24.6 us
  transfers between devices with their start and end apart: 14, of which 12 were waited for; matrix products, arithmetic and copies ran while one was open for 25% of the time, Pallas kernels for 0%

profile of v1, /device:TPU:0, one launch (start us, length us, event | category | flops | bytes accessed | tf_op | source)
XLA Modules:
  0.0 1154.8 jit_solution(671203548161399884)
XLA Ops:
  26.8 16.7 %all-to-all-done = bf16[2,4,197,384]{3,0,2,1:T(2,128)(2,1)S(1)} async-done(((bf16[2,4,197,384]{3,0,2,1:T(2,128)(2,1)}), bf16[2,4,197,384]{3,0,2,1:T(2,128)(2,1)S(1)}, u32[]{:S(2)}, u32[]{:S(2)}) %all-to-all-start) | async-done | bytes 1210400 | tf_op jit(solution)/shard_map/all_to_all | solution.py:132
  49.5 28.8 %all-gather.18.cloned.1.call-done = bf16[6144,384]{1,0:T(8,128)(2,1)} async-done(((bf16[192,384]{1,0:T(8,128)(2,1)}), bf16[6144,384]{1,0:T(8,128)(2,1)}) %all-gather.18.cloned.1.call-update) | async-done | bytes 4718608 | tf_op jit(solution)/shard_map/all_gather | solution.py:99
  95.5 50.8 %all-gather.22.cloned.1.call-done = bf16[32,210,384]{2,1,0:T(8,128)(2,1)} async-done(((bf16[1,210,384]{2,1,0:T(8,128)(2,1)}), bf16[32,210,384]{2,1,0:T(8,128)(2,1)}) %all-gather.22.cloned.1.call-update) | async-done | bytes 5160976 | tf_op jit(solution)/shard_map/all_gather | solution.py:99
  198.2 32.6 %all-gather.20.cloned.1.call-done = bf16[12288,384]{1,0:T(8,128)(2,1)} async-done(((bf16[384,384]{1,0:T(8,128)(2,1)}), bf16[12288,384]{1,0:T(8,128)(2,1)}) %all-gather.20.cloned.1.call-update) | async-done | bytes 9437200 | tf_op jit(solution)/shard_map/all_gather | solution.py:106
  230.8 9.0 fusion.96
  239.8 9.5 copy.577
  254.9 59.8 %all-gather.16.cloned.1.call-done = bf16[12288,384]{1,0:T(8,128)(2,1)} async-done(((bf16[384,384]{1,0:T(8,128)(2,1)}), bf16[12288,384]{1,0:T(8,128)(2,1)}) %all-gather.16.cloned.1.call-update) | async-done | bytes 9437200 | tf_op jit(solution)/shard_map/all_gather | solution.py:106
  314.8 9.0 fusion.97
  323.8 9.4 copy.574
  338.5 9.5 copy.573
  353.5 9.4 copy.578
  368.7 16.5 %multiply_convert_fusion.3 = (bf16[416,3072]{1,0:T(8,128)(2,1)S(1)}, f32[416,3072]{1,0:T(8,128)}, f32[416,3072]{1,0:T(8,128)}) fusion(f32[3072]{0:T(1024)S(1)} %bitcast.504, bf16[3072,768]{1,0:T(8,128)(2,1)S(1)} %bitcast.421, f32[416,768]{1,0:T(8,128)S(1)} %copy-done.17, f32[768]{0:T(1024)S(1)} %get-tuple-element.112, f32[768]{0:T(1024)S(1)} %get-tuple-element.108, ...), kind=kOutput, calls=%fused_computation.31 | convolution fusion | flops 2048876544 | bytes 18797824 | tf_op jit(solution)/shard_map/td,fd->tf/dot_general | solution.py:44
  417.3 15.7 %convert_reduce_fusion = (f32[3072]{0:T(1024)S(1)}, bf16[416,3072]{1,0:T(8,128)(2,1)S(1)}, f32[416,3072]{1,0:T(8,128)S(1)}) fusion(f32[416,3072]{1,0:T(8,128)S(1)} %fusion.90, f32[3072]{0:T(1024)S(1)} %bitcast.502, bf16[416,768]{1,0:T(8,128)(2,1)S(1)} %bitcast.455, bf16[3072,768]{1,0:T(8,128)(2,1)S(1)} %bitcast.417), kind=kOutput, calls=%fused_computation.8 | convolution fusion | flops 2058777600 | bytes 18161664 | tf_op jit(solution)/shard_map/td,fd->tf/dot_general | solution.py:44
  439.1 10.3 reshape.737
  459.3 10.2 reshape.739
  527.6 10.2 reshape.732
  547.8 10.1 reshape.734
  661.7 91.2 %reduce-scatter.9.cloned.1.call-done = bf16[1,384,384]{2,1,0:T(8,128)(2,1)} async-done(((bf16[32,384,384]{2,1,0:T(8,128)(2,1)}), bf16[1,384,384]{2,1,0:T(8,128)(2,1)}) %reduce-scatter.9.cloned.1.call-update) | async-done | bytes 294928 | tf_op jit(solution)/shard_map/reduce_scatter | solution.py:126
  752.9 123.6 %all-reduce.3.cloned.1.call-done = f32[18432]{0:T(1024)} async-done(((f32[18432]{0:T(1024)}), f32[18432]{0:T(1024)}) %all-reduce.3.cloned.1.call-update) | async-done | bytes 73744 | tf_op jit(solution)/shard_map/psum | solution.py:260
  886.5 8.5 all-to-all-done.2
  899.3 91.5 %reduce-scatter.7.cloned.1.call-done = bf16[1,192,384]{2,1,0:T(8,128)(2,1)} async-done(((bf16[32,192,384]{2,1,0:T(8,128)(2,1)}), bf16[1,192,384]{2,1,0:T(8,128)(2,1)}) %reduce-scatter.7.cloned.1.call-update) | async-done | bytes 147472 | tf_op jit(solution)/shard_map/reduce_scatter | solution.py:126
  998.6 104.7 %reduce-scatter.5.cloned.1.call-done = bf16[1,192,384]{2,1,0:T(8,128)(2,1)} async-done(((bf16[32,192,384]{2,1,0:T(8,128)(2,1)}), bf16[1,192,384]{2,1,0:T(8,128)(2,1)}) %reduce-scatter.5.cloned.1.call-update) | async-done | bytes 147472 | tf_op jit(solution)/shard_map/reduce_scatter | solution.py:126
  1113.4 7.9 all-gather.14.cloned.1.call-done
  1123.7 16.6 %all-gather.12.cloned.1.call-done = bf16[4,384,384]{2,1,0:T(8,128)(2,1)} async-done(((bf16[1,384,384]{2,1,0:T(8,128)(2,1)}), bf16[4,384,384]{2,1,0:T(8,128)(2,1)}) %all-gather.12.cloned.1.call-update) | async-done | bytes 1179664 | tf_op jit(solution)/shard_map/all_gather | solution.py:279
  (558 shorter events, 376.4 us)
Async XLA Ops:
  7.2 71.2 %all-gather.18.cloned.1.call-start = ((), (), s32[]{:S(2)}) async-start(), calls=%async_computation.15 | async-start | bytes 4866048 | tf_op jit(solution)/shard_map/all_gather | solution.py:99
  11.9 134.4 %all-gather.22.cloned.1.call-start = ((), (), s32[]{:S(2)}) async-start(), calls=%async_computation.17 | async-start | bytes 5474304 | tf_op jit(solution)/shard_map/all_gather | solution.py:99
  16.1 214.6 %all-gather.20.cloned.1.call-start = ((), (), s32[]{:S(2)}) async-start(), calls=%async_computation.16 | async-start | bytes 9732096 | tf_op jit(solution)/shard_map/all_gather | solution.py:106
  18.9 295.9 %all-gather.16.cloned.1.call-start = ((), (), s32[]{:S(2)}) async-start(), calls=%async_computation.14 | async-start | bytes 9732096 | tf_op jit(solution)/shard_map/all_gather | solution.py:106
  22.3 21.2 %all-to-all-start = ((bf16[2,4,197,384]{3,0,2,1:T(2,128)(2,1)}), bf16[2,4,197,384]{3,0,2,1:T(2,128)(2,1)S(1)}, u32[]{:S(2)}, u32[]{:S(2)}) async-start(bf16[2,4,197,384]{3,0,2,1:T(2,128)(2,1)} %copy.451), calls=%async_computation | async-start | bytes 2420736 | tf_op jit(solution)/shard_map/all_to_all | solution.py:132
  26.6 619.4 %reduce-scatter.11.cloned.1.call-start = ((), (), s32[]{:S(2)}) async-start(), calls=%async_computation.12 | async-start | bytes 9732096 | tf_op jit(solution)/shard_map/reduce_scatter | solution.py:126
  46.6 120.5 %copy-start = (bf16[2,2,197,768]{3,2,1,0:T(8,128)(2,1)}, bf16[2,2,197,768]{3,2,1,0:T(8,128)(2,1)S(1)}, u32[]{:S(2)}) copy-start(bf16[2,2,197,768]{3,2,1,0:T(8,128)(2,1)S(1)} %all_to_all.36) | copy-start | bytes 3631108
  49.5 117.5 %copy-start.83 = (f32[2,208]{1,0:T(2,128)}, f32[2,208]{1,0:T(2,128)S(1)}, u32[]{:S(2)}) copy-start(f32[2,208]{1,0:T(2,128)S(1)} %get-tuple-element.164) | copy-start | bytes 4996
  167.0 201.6 %copy-start.96 = (f32[768]{0:T(1024)}, f32[768]{0:T(1024)S(1)}, u32[]{:S(2)}) copy-start(f32[768]{0:T(1024)S(1)} %get-tuple-element.112) | copy-start | bytes 9220
  167.0 220.6 %copy-start.75 = (f32[768]{0:T(1024)}, f32[768]{0:T(1024)S(1)}, u32[]{:S(2)}) copy-start(f32[768]{0:T(1024)S(1)} %get-tuple-element.111) | copy-start | bytes 9220
  167.1 201.5 %copy-start.85 = (f32[768]{0:T(1024)}, f32[768]{0:T(1024)S(1)}, u32[]{:S(2)}) copy-start(f32[768]{0:T(1024)S(1)} %get-tuple-element.108) | copy-start | bytes 9220
  167.1 220.6 %copy-start.71 = (f32[768]{0:T(1024)}, f32[768]{0:T(1024)S(1)}, u32[]{:S(2)}) copy-start(f32[768]{0:T(1024)S(1)} %get-tuple-element.107) | copy-start | bytes 9220
  194.3 45.4 %copy-start.35 = (bf16[416,768]{0,1:T(8,128)(2,1)}, bf16[416,768]{0,1:T(8,128)(2,1)S(1)}, u32[]{:S(2)}) copy-start(bf16[416,768]{0,1:T(8,128)(2,1)S(1)} %reshape.684) | copy-start | bytes 1916932
  198.1 170.5 %copy-start.90 = (f32[416]{0:T(512)}, f32[416]{0:T(512)S(1)}, u32[]{:S(2)}) copy-start(f32[416]{0:T(512)S(1)} %get-tuple-element.169) | copy-start | bytes 4996
  198.1 170.5 %copy-start.92 = (f32[416]{0:T(512)}, f32[416]{0:T(512)S(1)}, u32[]{:S(2)}) copy-start(f32[416]{0:T(512)S(1)} %get-tuple-element.170) | copy-start | bytes 4996
  198.2 170.4 %copy-start.88 = (f32[1,4,768]{2,0,1:T(1,128)}, f32[1,4,768]{2,0,1:T(1,128)S(1)}, u32[]{:S(2)}) copy-start(f32[1,4,768]{2,0,1:T(1,128)S(1)} %get-tuple-element.161) | copy-start | bytes 36868
  477.3 275.6 %reduce-scatter.9.cloned.1.call-start = ((), (), s32[]{:S(2)}) async-start(), calls=%async_computation.10 | async-start | bytes 9732096 | tf_op jit(solution)/shard_map/reduce_scatter | solution.py:126
  568.0 308.5 %all-reduce.3.cloned.1.call-start = ((), (), s32[]{:S(2)}) async-start(), calls=%async_computation.7 | async-start | bytes 147456 | tf_op jit(solution)/shard_map/psum | solution.py:260
  622.9 367.9 %reduce-scatter.7.cloned.1.call-start = ((), (), s32[]{:S(2)}) async-start(), calls=%async_computation.9 | async-start | bytes 4866048 | tf_op jit(solution)/shard_map/reduce_scatter | solution.py:126
  628.4 474.9 %reduce-scatter.5.cloned.1.call-start = ((), (), s32[]{:S(2)}) async-start(), calls=%async_computation.8 | async-start | bytes 4866048 | tf_op jit(solution)/shard_map/reduce_scatter | solution.py:126
  645.9 475.4 %all-gather.14.cloned.1.call-start = ((), (), s32[]{:S(2)}) async-start(), calls=%async_computation.13 | async-start | bytes 1474560 | tf_op jit(solution)/shard_map/all_gather | solution.py:279
  654.4 225.1 %all-to-all-start.1 = ((bf16[2,197,768]{1,0,2:T(2,128)(2,1)}), bf16[2,197,768]{1,0,2:T(2,128)(2,1)S(1)}, u32[]{:S(2)}, u32[]{:S(2)}) async-start(bf16[2,197,768]{1,0,2:T(2,128)(2,1)} %copy.579), calls=%async_computation.1 | async-start | bytes 1572864 | tf_op jit(solution)/shard_map/all_to_all | solution.py:137
  658.0 482.4 %all-gather.12.cloned.1.call-start = ((), (), s32[]{:S(2)}) async-start(), calls=%async_computation.11 | async-start | bytes 1474560 | tf_op jit(solution)/shard_map/all_gather | solution.py:279
  879.5 15.5 %all-to-all-start.2 = ((bf16[2,197,768]{1,0,2:T(2,128)(2,1)}), bf16[2,197,768]{1,0,2:T(2,128)(2,1)S(1)}, u32[]{:S(2)}, u32[]{:S(2)}) async-start(bf16[2,197,768]{1,0,2:T(2,128)(2,1)} %copy.580), calls=%async_computation.2 | async-start | bytes 1572864 | tf_op jit(solution)/shard_map/all_to_all | solution.py:137
  (113 other events, 528.1 us)
Sparse Core Ops, SparseCore 0:
  12.0 66.3 all-gather.17
  81.8 64.4 all-gather.21
  149.8 80.8 all-gather.19
  234.1 80.6 all-gather.15
  477.4 134.1 reduce-scatter.10
  618.3 134.5 reduce-scatter.8
  759.1 117.3 all-reduce.2
  882.0 108.8 reduce-scatter.6
  997.2 106.0 reduce-scatter.4
  1104.7 16.5 all-gather.13
  1122.9 17.4 all-gather.11
